TPU v7x, 512 devices: a whole 4x4x16 slice. The times are simulated.
512 devices in a mesh: grp: 64 (over x, z), dev: 8 (over y, core).
Axes of the slice: x: 4, y: 4, z: 16, core: 2. Of those that a mesh axis runs over, the one named last changes fastest.
Arguments:
- tokens: bfloat16 [32768, 768], P(('grp', 'dev')), may hold values from -6 to 6
- expert_ids: int32 [32768, 8], P(('grp', 'dev')), may hold values from 0 to 511, as said below
- gates: bfloat16 [32768, 8], P(('grp', 'dev')), may hold values from 0.099609375 to 0.5
- w_in: bfloat16 [512, 768, 1536], P(('grp', 'dev')), may hold values from -0.21875 to 0.21875
- w_out: bfloat16 [512, 1536, 768], P(('grp', 'dev')), may hold values from -0.15625 to 0.15625
Outputs:
- mixed: bfloat16 [32768, 768], P(('grp', 'dev'))
Inputs may be any that keep to these rules, and one draw needn't show every extreme that they name: `expert_ids`: row t lists 8 experts; columns 2 * k and 2 * k + 1 are two different experts of one group (experts g * 8 to g * 8 + 7 form group g), and the four groups of a row differ. The owner of token t is t // 64, and its dev index is the owner modulo 8. The tokens of one owner pick one group at most 12 times, and every owner reaches it for some group. The tokens whose owners share a dev index pick each group exactly 4 * 64 times in all and each expert at most 192 times; in every group one expert is picked 192 times by the tokens of every dev index.
All inputs are finite; a program needn't handle non-finite values.
Results may differ from a plain program's by a relative error of at most 0.0057.
Values may be sent and summed in bfloat16 or wider, within the bound.
A program may use at most 64 MiB of HBM per device.

v0:
```python
import jax
import jax.numpy as jnp
from jax import lax
from jax.sharding import PartitionSpec as P


def earlier_count(onehot):
    return jnp.cumsum(onehot, axis=0) - onehot


def contract_rows(left, right):
    return lax.dot_general(
        left,
        right,
        (((0,), (0,)), ((), ())),
        precision=lax.Precision.HIGHEST,
        preferred_element_type=jnp.float32,
    )


def expert_rows(slot_block, w_first, w_second):

    def one_block(rows_block):
        hidden = jnp.maximum(
            jnp.dot(rows_block, w_first, preferred_element_type=jnp.float32), 0.0
        ).astype(jnp.bfloat16)
        return jnp.dot(hidden, w_second, preferred_element_type=jnp.float32).astype(jnp.bfloat16)

    return lax.map(one_block, slot_block)


def seat_sources(seat_of, valid, seat_total):
    item_count = seat_of.shape[0]
    target_seat = jnp.where(valid, seat_of, seat_total)
    empty_seats = jnp.full((seat_total,), item_count, jnp.int32)
    return empty_seats.at[target_seat].set(jnp.arange(item_count, dtype=jnp.int32), mode="drop")


def per_device(tokens, expert_ids, gates, w_in, w_out):
    n_grp = lax.axis_size("grp")
    n_dev = lax.axis_size("dev")
    token_count, feature_width = tokens.shape
    cap_grp = min(token_count, 3 * ((4 * token_count + n_grp - 1) // n_grp))
    cap_exp = min(4 * token_count, 24 * token_count // n_dev)
    seat_total = n_dev * cap_exp
    zero_half = jnp.zeros((), jnp.bfloat16)
    w_first = w_in[0]
    w_second = w_out[0]
    pair_ids = expert_ids.reshape(token_count * 4, 2)
    pair_group = pair_ids[:, 0] // n_dev
    group_hot = (pair_group[:, None] == jnp.arange(n_grp)[None, :]).astype(jnp.int32)
    group_rank = jnp.sum(earlier_count(group_hot) * group_hot, axis=1)
    target = pair_group * cap_grp + group_rank
    slot_count = n_grp * cap_grp
    placed = (target[None, :] == jnp.arange(slot_count)[:, None]).astype(jnp.int32)
    token_hot = placed.reshape(slot_count, token_count, 4).sum(axis=2)
    rows_out = jnp.dot(
        token_hot.astype(jnp.bfloat16), tokens, preferred_element_type=jnp.float32
    ).astype(jnp.bfloat16)
    local_ids = pair_ids % n_dev
    picks_out = jnp.dot(placed, local_ids + 1) - 1
    gains_out = jnp.dot(
        placed.astype(jnp.bfloat16),
        gates.reshape(token_count * 4, 2),
        preferred_element_type=jnp.float32,
    ).astype(jnp.bfloat16)
    rows_in, picks_in, gains_in = (
        lax.all_to_all(
            rows_out.reshape(n_grp, cap_grp, feature_width),
            "grp",
            split_axis=0,
            concat_axis=0,
            tiled=True,
        ),
        lax.all_to_all(
            picks_out.reshape(n_grp, cap_grp, 2), "grp", split_axis=0, concat_axis=0, tiled=True
        ),
        lax.all_to_all(
            gains_out.reshape(n_grp, cap_grp, 2), "grp", split_axis=0, concat_axis=0, tiled=True
        ),
    )
    relay_rows = rows_in.reshape(slot_count, feature_width)
    relay_picks = picks_in.reshape(slot_count, 2)
    relay_gains = gains_in.reshape(slot_count, 2)
    live_count = 4 * token_count
    slot_live = (relay_picks[:, 0] >= 0).astype(jnp.int32)
    slot_order = jnp.cumsum(slot_live) - 1
    packed = (
        (slot_order[None, :] == jnp.arange(live_count)[:, None]) & (slot_live[None, :] > 0)
    ).astype(jnp.int32)
    packed_rows = jnp.dot(
        packed.astype(jnp.bfloat16), relay_rows, preferred_element_type=jnp.float32
    ).astype(jnp.bfloat16)
    packed_picks = jnp.dot(packed, relay_picks)
    packed_gains = jnp.dot(
        packed.astype(jnp.bfloat16), relay_gains, preferred_element_type=jnp.float32
    ).astype(jnp.bfloat16)
    group_rows, group_picks, group_gains = (
        lax.all_gather(packed_rows, "dev", axis=0, tiled=True),
        lax.all_gather(packed_picks, "dev", axis=0, tiled=True),
        lax.all_gather(packed_gains, "dev", axis=0, tiled=True),
    )
    gathered_count = group_rows.shape[0]
    chosen = jnp.sum((group_picks == lax.axis_index("dev")).astype(jnp.int32), axis=1)
    expert_seat = jnp.cumsum(chosen) - 1
    seat_source = seat_sources(expert_seat, chosen > 0, seat_total)
    seat_live = seat_source < gathered_count
    taken_rows = jnp.take(group_rows, jnp.minimum(seat_source, gathered_count - 1), axis=0)
    expert_in = jnp.where(seat_live[:, None], taken_rows, zero_half)
    expert_out = expert_rows(
        expert_in.reshape(n_dev, cap_exp, feature_width), w_first, w_second
    ).reshape(seat_total, feature_width)
    spread_rows = jnp.take(expert_out, jnp.clip(expert_seat, 0, seat_total - 1), axis=0)
    spread = jnp.where((chosen > 0)[:, None], spread_rows, zero_half)
    back = lax.all_to_all(
        spread.reshape(n_dev, live_count, feature_width),
        "dev",
        split_axis=0,
        concat_axis=0,
        tiled=True,
    )
    match = (packed_picks[None, :, :] == jnp.arange(n_dev)[:, None, None]).astype(jnp.float32)
    row_weights = jnp.sum(match * packed_gains.astype(jnp.float32)[None, :, :], axis=2)
    packed_sum = jnp.sum(row_weights[:, :, None] * back.astype(jnp.float32), axis=0)
    partial_value = contract_rows(packed.astype(jnp.float32), packed_sum)
    returned_sums = lax.all_to_all(
        partial_value.reshape(n_grp, cap_grp, feature_width),
        "grp",
        split_axis=0,
        concat_axis=0,
        tiled=True,
    )
    mixed = contract_rows(
        token_hot.astype(jnp.float32), returned_sums.reshape(slot_count, feature_width)
    )
    return mixed.astype(jnp.bfloat16)


def solution(mesh):
    return jax.shard_map(
        per_device,
        mesh=mesh,
        in_specs=(
            P(("grp", "dev"), None),
            P(("grp", "dev"), None),
            P(("grp", "dev"), None),
            P(("grp", "dev"), None, None),
            P(("grp", "dev"), None, None),
        ),
        out_specs=P(("grp", "dev"), None),
        check_vma=False,
    )
```

profile of v0, /device:TPU:6, one launch (start us, length us, event | category | flops | bytes accessed | tf_op | source)
XLA Modules:
  0.0 426.4 jit_solution(9296313556347692572)
XLA Ops:
  10.0 18.8 %all-to-all-start = ((s32[64,12,2]{1,2,0:T(2,128)}), s32[64,12,2]{1,2,0:T(2,128)S(1)}, u32[]{:S(2)}, u32[]{:S(2)}) async-start(s32[64,12,2]{1,2,0:T(2,128)} %copy.43), calls=%async_computation | async-start | bytes 131072 | tf_op jit(solution)/shard_map/all_to_all | solution.py:75
  31.1 10.6 %all-to-all-done = s32[64,12,2]{1,2,0:T(2,128)S(1)} async-done(((s32[64,12,2]{1,2,0:T(2,128)}), s32[64,12,2]{1,2,0:T(2,128)S(1)}, u32[]{:S(2)}, u32[]{:S(2)}) %all-to-all-start) | async-done | bytes 6176 | tf_op jit(solution)/shard_map/all_to_all | solution.py:75
  41.7 6.4 %all-to-all-start.2 = ((bf16[64,12,768]{2,1,0:T(8,128)(2,1)}), bf16[64,12,768]{2,1,0:T(8,128)(2,1)S(1)}, u32[]{:S(2)}, u32[]{:S(2)}) async-start(bf16[64,12,768]{2,1,0:T(8,128)(2,1)} %reshape.303), calls=%async_computation.2 | async-start | bytes 3145728 | tf_op jit(solution)/shard_map/all_to_all | solution.py:68
  48.9 74.3 %all-to-all-done.2 = bf16[64,12,768]{2,1,0:T(8,128)(2,1)S(1)} async-done(((bf16[64,12,768]{2,1,0:T(8,128)(2,1)}), bf16[64,12,768]{2,1,0:T(8,128)(2,1)S(1)}, u32[]{:S(2)}, u32[]{:S(2)}) %all-to-all-start.2) | async-done | bytes 1179680 | tf_op jit(solution)/shard_map/all_to_all | solution.py:68
  126.0 6.9 %all-to-all-start.1 = ((bf16[64,12,2]{1,2,0:T(2,128)(2,1)}), bf16[64,12,2]{1,2,0:T(2,128)(2,1)S(1)}, u32[]{:S(2)}, u32[]{:S(2)}) async-start(bf16[64,12,2]{1,2,0:T(2,128)(2,1)} %copy.48), calls=%async_computation.1 | async-start | bytes 65536 | tf_op jit(solution)/shard_map/all_to_all | solution.py:78
  133.5 12.1 %all_gather.6 = s32[2048,2]{0,1:T(2,128)S(1)} all-gather(s32[256,2]{0,1:T(2,128)S(1)} %fusion.19), channel_id=1, replica_groups=mesh['grp'=64,'dev'=8] {'dev'}, dimensions={0}, use_global_device_ids=true | all-gather | bytes 18432 | tf_op jit(solution)/shard_map/all_gather | solution.py:100
  146.4 8.0 %scatter_custom_fusion = s32[1536]{0:T(1024)S(1)} fusion(s32[2048]{0:T(1024)S(1)} %bitcast.90, s32[2048]{0:T(1024)S(1)} %iota.29, s32[]{:T(128)} %constant.103.clone.1), kind=kCustom, calls=%fused_computation.109 | custom fusion | bytes 6148 | tf_op jit(solution)/shard_map/scatter | solution.py:36
  154.8 9.0 %gather_fusion = bf16[1536,768]{1,0:T(8,128)(2,1)} fusion(bf16[2048,768]{1,0:T(8,128)(2,1)} %all-gather.2.cloned.1.call-done, s32[2048]{0:T(1024)S(1)} %pad_clamp_fusion), kind=kCustom, calls=%fused_computation | custom fusion | bytes 4724736 | tf_op jit(solution)/shard_map/jit(_take)/gather | solution.py:108
  163.8 3.0 select_select_fusion.1
  166.8 29.7 %while.11 = (s32[]{:T(128)}, bf16[8,192,768]{2,1,0:T(8,128)(2,1)S(1)}, bf16[8,192,768]{2,1,0:T(8,128)(2,1)}, bf16[768,1536]{1,0:T(8,128)(2,1)}, bf16[1536,768]{1,0:T(8,128)(2,1)}) while((s32[]{:T(128)}, bf16[8,192,768]{2,1,0:T(8,128)(2,1)S(1)}, bf16[8,192,768]{2,1,0:T(8,128)(2,1)}, bf16[768,1536]{1,0:T(8,128)(2,1)}, ...), condition=%wide.region_12.13_spmd.clone, body=%wide.region_11.12_spmd.sunk.clone | while | flops 906706944 | bytes 5309509 | solution.py:29
  166.8 3.7 fusion.84
  170.5 3.7 fusion.84
  174.2 3.7 fusion.84
  177.9 3.7 fusion.84
  181.7 3.7 fusion.84
  185.4 3.7 fusion.84
  189.1 3.7 fusion.84
  192.8 3.7 fusion.84
  196.5 9.4 %gather_fusion.1 = bf16[2048,768]{1,0:T(8,128)(2,1)} fusion(bf16[1536,768]{1,0:T(8,128)(2,1)S(1)} %bitcast.82, s32[2048]{0:T(1024)S(1)} %broadcast_clamp_fusion), kind=kCustom, calls=%fused_computation.1 | custom fusion | bytes 6299648 | tf_op jit(solution)/shard_map/jit(_take)/gather | solution.py:113
  205.9 3.5 select_select_fusion
  209.3 3.8 all-to-all-start.3
  214.0 37.3 %all-to-all-done.3 = bf16[8,256,768]{2,1,0:T(8,128)(2,1)S(1)} async-done(((bf16[8,256,768]{2,1,0:T(8,128)(2,1)}), bf16[8,256,768]{2,1,0:T(8,128)(2,1)S(1)}, u32[]{:S(2)}, u32[]{:S(2)}) %all-to-all-start.3) | async-done | bytes 3145760 | tf_op jit(solution)/shard_map/all_to_all | solution.py:115
  255.7 158.5 %all_to_all.25 = f32[64,12,768]{2,1,0:T(8,128)S(1)} all-to-all(f32[64,12,768]{2,1,0:T(8,128)S(1)} %copy.51), channel_id=1, replica_groups=mesh['grp'=64,'dev'=8] {'grp'}, dimensions={0} | all-to-all | bytes 4718592 | tf_op jit(solution)/shard_map/all_to_all | solution.py:126
  415.7 3.9 convolution_convert_fusion.3
  (79 shorter events, 17.6 us)
Async XLA Ops:
  6.5 22.8 %copy-start = (bf16[64,768]{1,0:T(8,128)(2,1)S(1)}, bf16[64,768]{1,0:T(8,128)(2,1)}, u32[]{:S(2)}) copy-start(bf16[64,768]{1,0:T(8,128)(2,1)} %param.7) | copy-start | bytes 294916
  10.0 31.7 %all-to-all-start = ((s32[64,12,2]{1,2,0:T(2,128)}), s32[64,12,2]{1,2,0:T(2,128)S(1)}, u32[]{:S(2)}, u32[]{:S(2)}) async-start(s32[64,12,2]{1,2,0:T(2,128)} %copy.43), calls=%async_computation | async-start | bytes 131072 | tf_op jit(solution)/shard_map/all_to_all | solution.py:75
  41.7 81.5 %all-to-all-start.2 = ((bf16[64,12,768]{2,1,0:T(8,128)(2,1)}), bf16[64,12,768]{2,1,0:T(8,128)(2,1)S(1)}, u32[]{:S(2)}, u32[]{:S(2)}) async-start(bf16[64,12,768]{2,1,0:T(8,128)(2,1)} %reshape.303), calls=%async_computation.2 | async-start | bytes 3145728 | tf_op jit(solution)/shard_map/all_to_all | solution.py:68
  48.2 106.7 %all-gather.2.cloned.1.call-start = ((), (), s32[]{:S(2)}) async-start(), calls=%async_computation.5 | async-start | bytes 3538944 | tf_op jit(solution)/shard_map/all_gather | solution.py:99
  48.9 75.8 %copy-start.1 = (bf16[64,8]{0,1:T(8,128)(2,1)S(1)}, bf16[64,8]{0,1:T(8,128)(2,1)}, u32[]{:S(2)}) copy-start(bf16[64,8]{0,1:T(8,128)(2,1)} %param.9) | copy-start | bytes 3076
  126.0 83.3 %all-to-all-start.1 = ((bf16[64,12,2]{1,2,0:T(2,128)(2,1)}), bf16[64,12,2]{1,2,0:T(2,128)(2,1)S(1)}, u32[]{:S(2)}, u32[]{:S(2)}) async-start(bf16[64,12,2]{1,2,0:T(2,128)(2,1)} %copy.48), calls=%async_computation.1 | async-start | bytes 65536 | tf_op jit(solution)/shard_map/all_to_all | solution.py:78
  209.3 42.0 %all-to-all-start.3 = ((bf16[8,256,768]{2,1,0:T(8,128)(2,1)}), bf16[8,256,768]{2,1,0:T(8,128)(2,1)S(1)}, u32[]{:S(2)}, u32[]{:S(2)}) async-start(bf16[8,256,768]{2,1,0:T(8,128)(2,1)} %select_select_fusion), calls=%async_computation.3 | async-start | bytes 6291456 | tf_op jit(solution)/shard_map/all_to_all | solution.py:115
Sparse Core Ops, SparseCore 0:
  124.9 28.0 all-gather.1
where the time goes:
time: 427 us; the launch traced here: 426 us
  blocking collectives  171 us (40%)
  waiting for transfers between devices  122 us (29%)
  matrix products  38.9 us (9%)
  starting transfers between devices  36 us (8%)
  local copies, waits for them, and re-layouts  35.5 us (8%)
  between operations  13.7 us (3%)
  other arithmetic  9.29 us (2%)
    all_to_all x1, blocking collectives, per_device(): lax.all_to_all(partial_value.reshape(n_grp, cap_grp, feature_width), 'grp...  159 us
    all_to_all x1, waiting for transfers between devices, per_device(): lax.all_to_all(rows_out.reshape(n_grp, cap_grp, feature_width), 'grp', sp...  74.3 us
    all_to_all x1, waiting for transfers between devices, per_device(): lax.all_to_all(spread.reshape(n_dev, live_count, feature_width), 'dev', s...  37.3 us
    dot_general x8, matrix products, one_block(): jnp.dot(hidden, w_second, preferred_element_type=jnp.float32)  29.5 us
    all_to_all x1, starting transfers between devices, per_device(): lax.all_to_all(picks_out.reshape(n_grp, cap_grp, 2), 'grp', split_axis=0,...  18.8 us
    all_gather x1, blocking collectives, per_device(): lax.all_gather(packed_picks, 'dev', axis=0, tiled=True)  12.1 us
    all_to_all x1, waiting for transfers between devices, per_device(): lax.all_to_all(picks_out.reshape(n_grp, cap_grp, 2), 'grp', split_axis=0,...  10.6 us
    gather x1, local copies, waits for them, and re-layouts, per_device(): jnp.take(expert_out, jnp.clip(expert_seat, 0, seat_total - 1), axis=0)  9.38 us
  transfers between devices with their start and end apart: 5, of which 3 were waited for; matrix products, arithmetic and copies ran while one was open for 16% of the time, Pallas kernels for 0%

commit v1 on v0

--- a/solution.py
+++ b/solution.py
@@ -97,7 +97,9 @@
     ).astype(jnp.bfloat16)
     group_rows, group_picks, group_gains = (
         lax.all_gather(packed_rows, "dev", axis=0, tiled=True),
-        lax.all_gather(packed_picks, "dev", axis=0, tiled=True),
+        jnp.concatenate(
+            lax.all_to_all(jnp.stack([packed_picks] * lax.axis_size("dev")), "dev", 0, 0), axis=0
+        ),
         lax.all_gather(packed_gains, "dev", axis=0, tiled=True),
     )
     gathered_count = group_rows.shape[0]

time: 427 us -> 426 us (level)
  blocking collectives: 171 us -> 159 us
  waiting for transfers between devices: 122 us -> 127 us
  starting transfers between devices: 36 us -> 40.4 us
    all_gather x1 -> x0, blocking collectives: 12.1 us -> none  [per_device(): lax.all_gather(packed_picks, 'dev', axis=0, tiled=True)]
    all_to_all x0 -> x1, starting transfers between devices: none -> 4.47 us  [per_device(): lax.all_to_all(jnp.stack([packed_picks] * lax.axis_size('dev')), 'dev', 0...]
    all_to_all x0 -> x1, waiting for transfers between devices: none -> 4.33 us  [per_device(): lax.all_to_all(jnp.stack([packed_picks] * lax.axis_size('dev')), 'dev', 0...]
  transfers between devices with their start and end apart: 5 -> 6, of which waited for: 3 -> 5; matrix products, arithmetic and copies ran while one was open for 16% -> 16% of each run, Pallas kernels for 0% -> 0%
where the time goes in v1:
time: 426 us; the launch traced here: 425 us
  blocking collectives  159 us (37%)
  waiting for transfers between devices  127 us (30%)
  starting transfers between devices  40.4 us (9%)
  matrix products  39 us (9%)
  local copies, waits for them, and re-layouts  36.1 us (8%)
  between operations  13.7 us (3%)
  other arithmetic  9.34 us (2%)
    all_to_all x1, blocking collectives, per_device(): lax.all_to_all(partial_value.reshape(n_grp, cap_grp, feature_width), 'grp...  159 us
    all_to_all x1, waiting for transfers between devices, per_device(): lax.all_to_all(rows_out.reshape(n_grp, cap_grp, feature_width), 'grp', sp...  74.3 us
    all_to_all x1, waiting for transfers between devices, per_device(): lax.all_to_all(spread.reshape(n_dev, live_count, feature_width), 'dev', s...  37.3 us
    dot_general x8, matrix products, one_block(): jnp.dot(hidden, w_second, preferred_element_type=jnp.float32)  29.5 us
    all_to_all x1, starting transfers between devices, per_device(): lax.all_to_all(picks_out.reshape(n_grp, cap_grp, 2), 'grp', split_axis=0,...  18.8 us
    all_to_all x1, waiting for transfers between devices, per_device(): lax.all_to_all(picks_out.reshape(n_grp, cap_grp, 2), 'grp', split_axis=0,...  10.6 us
    gather x1, local copies, waits for them, and re-layouts, per_device(): jnp.take(expert_out, jnp.clip(expert_seat, 0, seat_total - 1), axis=0)  9.38 us
    gather x1, local copies, waits for them, and re-layouts, per_device(): jnp.take(group_rows, jnp.minimum(seat_source, gathered_count - 1), axis=0)  8.99 us
  transfers between devices with their start and end apart: 6, of which 5 were waited for; matrix products, arithmetic and copies ran while one was open for 16% of the time, Pallas kernels for 0%

profile of v1, /device:TPU:6, one launch (start us, length us, event | category | flops | bytes accessed | tf_op | source)
XLA Modules:
  0.0 425.3 jit_solution(8544348209032621251)
XLA Ops:
  10.0 18.8 %all-to-all-start = ((s32[64,12,2]{1,2,0:T(2,128)}), s32[64,12,2]{1,2,0:T(2,128)S(1)}, u32[]{:S(2)}, u32[]{:S(2)}) async-start(s32[64,12,2]{1,2,0:T(2,128)} %copy.41), calls=%async_computation | async-start | bytes 131072 | tf_op jit(solution)/shard_map/all_to_all | solution.py:75
  31.1 10.6 %all-to-all-done = s32[64,12,2]{1,2,0:T(2,128)S(1)} async-done(((s32[64,12,2]{1,2,0:T(2,128)}), s32[64,12,2]{1,2,0:T(2,128)S(1)}, u32[]{:S(2)}, u32[]{:S(2)}) %all-to-all-start) | async-done | bytes 6176 | tf_op jit(solution)/shard_map/all_to_all | solution.py:75
  41.7 6.4 %all-to-all-start.3 = ((bf16[64,12,768]{2,1,0:T(8,128)(2,1)}), bf16[64,12,768]{2,1,0:T(8,128)(2,1)S(1)}, u32[]{:S(2)}, u32[]{:S(2)}) async-start(bf16[64,12,768]{2,1,0:T(8,128)(2,1)} %reshape.310), calls=%async_computation.3 | async-start | bytes 3145728 | tf_op jit(solution)/shard_map/all_to_all | solution.py:68
  48.9 74.3 %all-to-all-done.3 = bf16[64,12,768]{2,1,0:T(8,128)(2,1)S(1)} async-done(((bf16[64,12,768]{2,1,0:T(8,128)(2,1)}), bf16[64,12,768]{2,1,0:T(8,128)(2,1)S(1)}, u32[]{:S(2)}, u32[]{:S(2)}) %all-to-all-start.3) | async-done | bytes 1179680 | tf_op jit(solution)/shard_map/all_to_all | solution.py:68
  126.1 4.5 %all-to-all-start.2 = ((s32[8,256,2]{1,2,0:T(2,128)}), s32[8,256,2]{1,2,0:T(2,128)S(1)}, u32[]{:S(2)}, u32[]{:S(2)}) async-start(s32[8,256,2]{1,2,0:T(2,128)} %eq.108), calls=%async_computation.2 | async-start | bytes 32768 | tf_op jit(solution)/shard_map/all_to_all | solution.py:101
  131.6 4.3 %all-to-all-done.2 = s32[8,256,2]{1,2,0:T(2,128)S(1)} async-done(((s32[8,256,2]{1,2,0:T(2,128)}), s32[8,256,2]{1,2,0:T(2,128)S(1)}, u32[]{:S(2)}, u32[]{:S(2)}) %all-to-all-start.2) | async-done | bytes 16416 | tf_op jit(solution)/shard_map/all_to_all | solution.py:101
  136.0 6.9 %all-to-all-start.1 = ((bf16[64,12,2]{1,2,0:T(2,128)(2,1)}), bf16[64,12,2]{1,2,0:T(2,128)(2,1)S(1)}, u32[]{:S(2)}, u32[]{:S(2)}) async-start(bf16[64,12,2]{1,2,0:T(2,128)(2,1)} %copy.46), calls=%async_computation.1 | async-start | bytes 65536 | tf_op jit(solution)/shard_map/all_to_all | solution.py:78
  143.8 8.0 %scatter_custom_fusion = s32[1536]{0:T(1024)S(1)} fusion(s32[2048]{0:T(1024)S(1)} %bitcast.93, s32[2048]{0:T(1024)S(1)} %iota.29, s32[]{:T(128)} %constant.103.clone.1), kind=kCustom, calls=%fused_computation.108 | custom fusion | bytes 6148 | tf_op jit(solution)/shard_map/scatter | solution.py:36
  152.9 9.0 %gather_fusion = bf16[1536,768]{1,0:T(8,128)(2,1)} fusion(bf16[2048,768]{1,0:T(8,128)(2,1)} %all-gather.2.cloned.1.call-done, s32[2048]{0:T(1024)S(1)} %pad_clamp_fusion), kind=kCustom, calls=%fused_computation | custom fusion | bytes 4724736 | tf_op jit(solution)/shard_map/jit(_take)/gather | solution.py:110
  164.9 29.7 %while.11 = (s32[]{:T(128)}, bf16[8,192,768]{2,1,0:T(8,128)(2,1)S(1)}, bf16[8,192,768]{2,1,0:T(8,128)(2,1)}, bf16[768,1536]{1,0:T(8,128)(2,1)}, bf16[1536,768]{1,0:T(8,128)(2,1)}) while((s32[]{:T(128)}, bf16[8,192,768]{2,1,0:T(8,128)(2,1)S(1)}, bf16[8,192,768]{2,1,0:T(8,128)(2,1)}, bf16[768,1536]{1,0:T(8,128)(2,1)}, ...), condition=%wide.region_12.13_spmd.clone, body=%wide.region_11.12_spmd.sunk.clone | while | flops 906706944 | bytes 5309501 | solution.py:29
  164.9 3.7 fusion.85
  168.6 3.7 fusion.85
  172.3 3.7 fusion.85
  176.0 3.7 fusion.85
  179.7 3.7 fusion.85
  183.4 3.7 fusion.85
  187.1 3.7 fusion.85
  190.9 3.7 fusion.85
  194.6 9.4 %gather_fusion.1 = bf16[2048,768]{1,0:T(8,128)(2,1)} fusion(bf16[1536,768]{1,0:T(8,128)(2,1)S(1)} %bitcast.84, s32[2048]{0:T(1024)S(1)} %broadcast_clamp_fusion), kind=kCustom, calls=%fused_computation.1 | custom fusion | bytes 6299648 | tf_op jit(solution)/shard_map/jit(_take)/gather | solution.py:115
  203.9 3.5 select_select_fusion
  207.4 3.8 all-to-all-start.4
  212.1 37.3 %all-to-all-done.4 = bf16[8,256,768]{2,1,0:T(8,128)(2,1)S(1)} async-done(((bf16[8,256,768]{2,1,0:T(8,128)(2,1)}), bf16[8,256,768]{2,1,0:T(8,128)(2,1)S(1)}, u32[]{:S(2)}, u32[]{:S(2)}) %all-to-all-start.4) | async-done | bytes 3145760 | tf_op jit(solution)/shard_map/all_to_all | solution.py:117
  253.7 159.3 %all_to_all.30 = f32[64,12,768]{2,1,0:T(8,128)S(1)} all-to-all(f32[64,12,768]{2,1,0:T(8,128)S(1)} %copy.49), channel_id=1, replica_groups=mesh['grp'=64,'dev'=8] {'grp'}, dimensions={0} | all-to-all | bytes 4718592 | tf_op jit(solution)/shard_map/all_to_all | solution.py:128
  414.6 3.8 convolution_convert_fusion.3
  (81 shorter events, 22.0 us)
Async XLA Ops:
  6.5 22.8 %copy-start = (bf16[64,768]{1,0:T(8,128)(2,1)S(1)}, bf16[64,768]{1,0:T(8,128)(2,1)}, u32[]{:S(2)}) copy-start(bf16[64,768]{1,0:T(8,128)(2,1)} %param.7) | copy-start | bytes 294916
  10.0 31.7 %all-to-all-start = ((s32[64,12,2]{1,2,0:T(2,128)}), s32[64,12,2]{1,2,0:T(2,128)S(1)}, u32[]{:S(2)}, u32[]{:S(2)}) async-start(s32[64,12,2]{1,2,0:T(2,128)} %copy.41), calls=%async_computation | async-start | bytes 131072 | tf_op jit(solution)/shard_map/all_to_all | solution.py:75
  41.7 81.5 %all-to-all-start.3 = ((bf16[64,12,768]{2,1,0:T(8,128)(2,1)}), bf16[64,12,768]{2,1,0:T(8,128)(2,1)S(1)}, u32[]{:S(2)}, u32[]{:S(2)}) async-start(bf16[64,12,768]{2,1,0:T(8,128)(2,1)} %reshape.310), calls=%async_computation.3 | async-start | bytes 3145728 | tf_op jit(solution)/shard_map/all_to_all | solution.py:68
  48.2 104.7 %all-gather.2.cloned.1.call-start = ((), (), s32[]{:S(2)}) async-start(), calls=%async_computation.6 | async-start | bytes 3538944 | tf_op jit(solution)/shard_map/all_gather | solution.py:99
  48.9 75.8 %copy-start.1 = (bf16[64,8]{0,1:T(8,128)(2,1)S(1)}, bf16[64,8]{0,1:T(8,128)(2,1)}, u32[]{:S(2)}) copy-start(bf16[64,8]{0,1:T(8,128)(2,1)} %param.9) | copy-start | bytes 3076
  126.1 9.8 %all-to-all-start.2 = ((s32[8,256,2]{1,2,0:T(2,128)}), s32[8,256,2]{1,2,0:T(2,128)S(1)}, u32[]{:S(2)}, u32[]{:S(2)}) async-start(s32[8,256,2]{1,2,0:T(2,128)} %eq.108), calls=%async_computation.2 | async-start | bytes 32768 | tf_op jit(solution)/shard_map/all_to_all | solution.py:101
  136.0 71.4 %all-to-all-start.1 = ((bf16[64,12,2]{1,2,0:T(2,128)(2,1)}), bf16[64,12,2]{1,2,0:T(2,128)(2,1)S(1)}, u32[]{:S(2)}, u32[]{:S(2)}) async-start(bf16[64,12,2]{1,2,0:T(2,128)(2,1)} %copy.46), calls=%async_computation.1 | async-start | bytes 65536 | tf_op jit(solution)/shard_map/all_to_all | solution.py:78
  207.4 42.0 %all-to-all-start.4 = ((bf16[8,256,768]{2,1,0:T(8,128)(2,1)}), bf16[8,256,768]{2,1,0:T(8,128)(2,1)S(1)}, u32[]{:S(2)}, u32[]{:S(2)}) async-start(bf16[8,256,768]{2,1,0:T(8,128)(2,1)} %select_select_fusion), calls=%async_computation.4 | async-start | bytes 6291456 | tf_op jit(solution)/shard_map/all_to_all | solution.py:117
Sparse Core Ops, SparseCore 0:
  124.9 27.9 all-gather.1
